TPU v7x, 256 devices: a whole 4x4x8 slice. The times are simulated.
256 devices in a mesh: pb: 64 (over z, x, core), ka: 4 (over y).
Axes of the slice: x: 4, y: 4, z: 8, core: 2. Of those that a mesh axis runs over, the one named last changes fastest.
Arguments:
- queries: bfloat16 [65536, 512], P('pb'), may hold values from -80 to 80
- key_cache: bfloat16 [65536, 128], P(('ka', 'pb')), may hold values from -4.1 to 4.1
- value_cache: bfloat16 [65536, 128], P(('ka', 'pb')), may hold values from -4 to 4
- block_list: int32 [512, 32], P('pb'), may hold values from 0 to 511, as said below
- block_count: int32 [512], P('pb'), may hold values from 1 to 32, as said below
Outputs:
- attended: bfloat16 [65536, 512], P(('pb', 'ka'))
Inputs may be any that keep to these rules, and one draw needn't show every extreme that they name: `block_list`: entries of row qb before block_count[qb] are distinct blocks at most qb, and qb itself is among them. They are the blocks v at most qb of one set of 16 vertical blocks, then the blocks qb - o at least 0 (and not already listed) of one set of 16 slash offsets; both sets contain 0 and lie below 128. Later entries equal qb. `block_count`: the number of distinct listed blocks of each query block.
All inputs are finite; a program needn't handle non-finite values.
Results may differ from a plain program's by a relative error of at most 0.0046.
Values may be sent and summed in bfloat16 or wider, within the bound.
A program may use at most 128 MiB of HBM per device.

v0:
```python
import math
import jax
import jax.numpy as jnp
from jax import lax
from jax.sharding import PartitionSpec as P

HD = 128
QH = 4
BLK = 128
LIST = 32
masked_score = -1e30


def merged(shard, axis, combine):
    everything = jax.tree.map(lambda part: lax.all_gather(part, axis), shard)
    initial = jax.tree.map(lambda part: part[0], everything)

    def lap(k, so_far):
        return combine(so_far, jax.tree.map(lambda part: part[k], everything))

    return lax.fori_loop(1, lax.axis_size(axis), lap, initial)


def combine(first, second):
    peak_first, sum_first, out_first = first
    peak_second, sum_second, out_second = second
    peak_both = jnp.maximum(peak_first, peak_second)
    factor_first = jnp.exp(peak_first - peak_both)
    factor_second = jnp.exp(peak_second - peak_both)
    sum_both = factor_first * sum_first + factor_second * sum_second
    out_both = (
        jnp.repeat(factor_first, HD, axis=1) * out_first
        + jnp.repeat(factor_second, HD, axis=1) * out_second
    )
    return (peak_both, sum_both, out_both)


def shards(queries, key_cache, value_cache, block_list, block_count):
    shard_keys, shard_values = (
        lax.all_gather(key_cache, "pb", axis=0, tiled=True),
        lax.all_gather(value_cache, "pb", axis=0, tiled=True),
    )
    group_index = lax.axis_index("pb")
    shard_index = lax.axis_index("ka")
    ka_width = lax.axis_size("ka")
    score_scale = 1.0 / math.sqrt(HD)
    shard_width = shard_keys.shape[0] // BLK
    local_blocks = queries.shape[0] // BLK
    first_block = shard_index * shard_width
    all_key_tiles = shard_keys.reshape(shard_width, BLK, HD)
    all_value_tiles = shard_values.reshape(shard_width, BLK, HD)
    slot_ids = jnp.arange(LIST, dtype=jnp.int32)
    position = jnp.arange(BLK, dtype=jnp.int32)

    def one_block(block_pos):
        query_rows = lax.dynamic_slice_in_dim(queries, block_pos * BLK, BLK, 0).reshape(BLK, QH, HD)
        listed = lax.dynamic_index_in_dim(block_list, block_pos, 0, keepdims=False)
        live_count = lax.dynamic_index_in_dim(block_count, block_pos, 0, keepdims=False)
        global_pos = group_index * local_blocks + block_pos
        live_slot = slot_ids < live_count
        local_ids = listed - first_block
        tile_live = live_slot & (local_ids >= 0) & (local_ids < shard_width)
        picked = jnp.clip(local_ids, 0, shard_width - 1)
        key_tiles = all_key_tiles[picked]
        value_tiles = all_value_tiles[picked]
        scores = (
            jnp.einsum("qhd,skd->hqsk", query_rows, key_tiles, preferred_element_type=jnp.float32)
            * score_scale
        )
        earlier = (listed < global_pos)[None, :, None]
        diagonal = (listed == global_pos)[None, :, None] & (
            position[None, None, :] <= position[:, None, None]
        )
        valid = tile_live[None, :, None] & (earlier | diagonal)
        masked = jnp.where(valid[None], scores, masked_score)
        peak_row = jnp.max(masked, axis=(2, 3))
        weights = jnp.where(valid[None], jnp.exp(scores - peak_row[..., None, None]), 0.0)
        weight_sum = jnp.sum(weights, axis=(2, 3))
        partial_out = jnp.einsum(
            "hqsk,skd->qhd",
            weights.astype(jnp.bfloat16),
            value_tiles,
            preferred_element_type=jnp.float32,
        )
        return (peak_row.T, weight_sum.T, partial_out.reshape(BLK, QH * HD))

    peaks, sums, outputs = lax.map(one_block, jnp.arange(local_blocks, dtype=jnp.int32))
    peaks = peaks.reshape(local_blocks * BLK, QH)
    sums = sums.reshape(local_blocks * BLK, QH)
    outputs = outputs.reshape(local_blocks * BLK, QH * HD)
    merged_peak, merged_sum, merged_out = merged((peaks, sums, outputs), "ka", combine)
    owned = merged_out.shape[0] // ka_width
    out_share = lax.dynamic_slice_in_dim(merged_out, shard_index * owned, owned, 0)
    sum_share = lax.dynamic_slice_in_dim(merged_sum, shard_index * owned, owned, 0)
    return (out_share / jnp.repeat(sum_share, HD, axis=1)).astype(jnp.bfloat16)


def solution(mesh):
    placed = (P("pb", None), P(("ka", "pb"), None), P(("ka", "pb"), None), P("pb", None), P("pb"))
    return jax.shard_map(
        shards, mesh=mesh, in_specs=placed, out_specs=P(("pb", "ka"), None), check_vma=False
    )
```

profile of v0, /device:TPU:1, one launch (start us, length us, event | category | flops | bytes accessed | tf_op | source)
XLA Modules:
  0.0 492.1 jit_solution(4541151159910000270)
XLA Ops:
  8.1 85.3 %all-gather.4.cloned.1.call-done = bf16[16384,128]{1,0:T(8,128)(2,1)} async-done(((bf16[256,128]{1,0:T(8,128)(2,1)}), bf16[16384,128]{1,0:T(8,128)(2,1)}) %all-gather.4.cloned.1.call-update) | async-done | bytes 4194320 | tf_op jit(solution)/shard_map/all_gather | solution.py:40
  93.3 79.1 %all-gather.6.cloned.1.call-done = bf16[16384,128]{1,0:T(8,128)(2,1)} async-done(((bf16[256,128]{1,0:T(8,128)(2,1)}), bf16[16384,128]{1,0:T(8,128)(2,1)}) %all-gather.6.cloned.1.call-update) | async-done | bytes 4194320 | tf_op jit(solution)/shard_map/all_gather | solution.py:41
  172.4 201.8 %while.37 = (s32[]{:T(128)}, f32[8,128,4]{1,2,0:T(4,128)S(1)}, f32[8,128,4]{1,2,0:T(4,128)S(1)}, f32[8,128,512]{2,1,0:T(8,128)}, s32[8]{0:T(128)S(1)}, /*index=5...) while((s32[]{:T(128)}, f32[8,128,4]{1,2,0:T(4,128)S(1)}, ...), condition=%wide.region_3.4_spmd.clone, body=%wide.region_0.3_spmd.clone.sunk | while | flops 1098400256 | bytes 69129872 | solution.py:87
  181.2 2.9 gather_fusion
  191.6 5.2 %fusion.41 = f32[128,4,128,1]{2,0,1,3:T(8,128)S(1)} fusion(f32[32,128,128,4]{2,1,3,0:T(8,128)} %copy-done, f32[4,128]{1,0:T(4,128)S(1)} %get-tuple-element.581, pred[128,32,128]{0,2,1:T(8,128)(4,1)S(1)} %or_and_fusion.2, bf16[32,128,128]{2,1,0:T(8,128)(2,1)S(1)} %gather_fusion.1), kind=kOutput, calls=%fused_computation.20.clone.1 | convolution fusion | flops 545259520 | bytes 10225664 | tf_op jit(solution)/shard_map/while/body/eval_jaxpr/hqsk,skd->qhd/dot_general | solution.py:79
  206.4 2.9 gather_fusion
  216.8 5.2 %fusion.41 = f32[128,4,128,1]{2,0,1,3:T(8,128)S(1)} fusion(f32[32,128,128,4]{2,1,3,0:T(8,128)} %copy-done, f32[4,128]{1,0:T(4,128)S(1)} %get-tuple-element.581, pred[128,32,128]{0,2,1:T(8,128)(4,1)S(1)} %or_and_fusion.2, bf16[32,128,128]{2,1,0:T(8,128)(2,1)S(1)} %gather_fusion.1), kind=kOutput, calls=%fused_computation.20.clone.1 | convolution fusion | flops 545259520 | bytes 10225664 | tf_op jit(solution)/shard_map/while/body/eval_jaxpr/hqsk,skd->qhd/dot_general | solution.py:79
  231.7 2.9 gather_fusion
  242.0 5.2 %fusion.41 = f32[128,4,128,1]{2,0,1,3:T(8,128)S(1)} fusion(f32[32,128,128,4]{2,1,3,0:T(8,128)} %copy-done, f32[4,128]{1,0:T(4,128)S(1)} %get-tuple-element.581, pred[128,32,128]{0,2,1:T(8,128)(4,1)S(1)} %or_and_fusion.2, bf16[32,128,128]{2,1,0:T(8,128)(2,1)S(1)} %gather_fusion.1), kind=kOutput, calls=%fused_computation.20.clone.1 | convolution fusion | flops 545259520 | bytes 10225664 | tf_op jit(solution)/shard_map/while/body/eval_jaxpr/hqsk,skd->qhd/dot_general | solution.py:79
  267.2 5.2 %fusion.41 = f32[128,4,128,1]{2,0,1,3:T(8,128)S(1)} fusion(f32[32,128,128,4]{2,1,3,0:T(8,128)} %copy-done, f32[4,128]{1,0:T(4,128)S(1)} %get-tuple-element.581, pred[128,32,128]{0,2,1:T(8,128)(4,1)S(1)} %or_and_fusion.2, bf16[32,128,128]{2,1,0:T(8,128)(2,1)S(1)} %gather_fusion.1), kind=kOutput, calls=%fused_computation.20.clone.1 | convolution fusion | flops 545259520 | bytes 10225664 | tf_op jit(solution)/shard_map/while/body/eval_jaxpr/hqsk,skd->qhd/dot_general | solution.py:79
  282.1 2.9 gather_fusion
  292.4 5.2 %fusion.41 = f32[128,4,128,1]{2,0,1,3:T(8,128)S(1)} fusion(f32[32,128,128,4]{2,1,3,0:T(8,128)} %copy-done, f32[4,128]{1,0:T(4,128)S(1)} %get-tuple-element.581, pred[128,32,128]{0,2,1:T(8,128)(4,1)S(1)} %or_and_fusion.2, bf16[32,128,128]{2,1,0:T(8,128)(2,1)S(1)} %gather_fusion.1), kind=kOutput, calls=%fused_computation.20.clone.1 | convolution fusion | flops 545259520 | bytes 10225664 | tf_op jit(solution)/shard_map/while/body/eval_jaxpr/hqsk,skd->qhd/dot_general | solution.py:79
  307.3 2.9 gather_fusion
  317.7 5.2 %fusion.41 = f32[128,4,128,1]{2,0,1,3:T(8,128)S(1)} fusion(f32[32,128,128,4]{2,1,3,0:T(8,128)} %copy-done, f32[4,128]{1,0:T(4,128)S(1)} %get-tuple-element.581, pred[128,32,128]{0,2,1:T(8,128)(4,1)S(1)} %or_and_fusion.2, bf16[32,128,128]{2,1,0:T(8,128)(2,1)S(1)} %gather_fusion.1), kind=kOutput, calls=%fused_computation.20.clone.1 | convolution fusion | flops 545259520 | bytes 10225664 | tf_op jit(solution)/shard_map/while/body/eval_jaxpr/hqsk,skd->qhd/dot_general | solution.py:79
  342.9 5.2 %fusion.41 = f32[128,4,128,1]{2,0,1,3:T(8,128)S(1)} fusion(f32[32,128,128,4]{2,1,3,0:T(8,128)} %copy-done, f32[4,128]{1,0:T(4,128)S(1)} %get-tuple-element.581, pred[128,32,128]{0,2,1:T(8,128)(4,1)S(1)} %or_and_fusion.2, bf16[32,128,128]{2,1,0:T(8,128)(2,1)S(1)} %gather_fusion.1), kind=kOutput, calls=%fused_computation.20.clone.1 | convolution fusion | flops 545259520 | bytes 10225664 | tf_op jit(solution)/shard_map/while/body/eval_jaxpr/hqsk,skd->qhd/dot_general | solution.py:79
  368.1 5.2 %fusion.41 = f32[128,4,128,1]{2,0,1,3:T(8,128)S(1)} fusion(f32[32,128,128,4]{2,1,3,0:T(8,128)} %copy-done, f32[4,128]{1,0:T(4,128)S(1)} %get-tuple-element.581, pred[128,32,128]{0,2,1:T(8,128)(4,1)S(1)} %or_and_fusion.2, bf16[32,128,128]{2,1,0:T(8,128)(2,1)S(1)} %gather_fusion.1), kind=kOutput, calls=%fused_computation.20.clone.1 | convolution fusion | flops 545259520 | bytes 10225664 | tf_op jit(solution)/shard_map/while/body/eval_jaxpr/hqsk,skd->qhd/dot_general | solution.py:79
  374.2 9.6 %all_gather.17 = f32[4,1024,4]{1,2,0:T(4,128)S(1)} all-gather(f32[1,1024,4]{1,2,0:T(4,128)S(1)} %bitcast.155), channel_id=1, replica_groups=mesh['pb'=64,'ka'=4] {'ka'}, dimensions={0}, use_global_device_ids=true | all-gather | bytes 81920 | tf_op jit(solution)/shard_map/all_gather | solution.py:15
  383.8 9.9 %all_gather.18 = f32[4,1024,4]{1,2,0:T(4,128)S(1)} all-gather(f32[1,1024,4]{1,2,0:T(4,128)S(1)} %bitcast.156), channel_id=1, replica_groups=mesh['pb'=64,'ka'=4] {'ka'}, dimensions={0}, use_global_device_ids=true | all-gather | bytes 81920 | tf_op jit(solution)/shard_map/all_gather | solution.py:15
  393.7 63.6 %all-gather.8.cloned.1.call-done = f32[4,1024,512]{2,1,0:T(8,128)} async-done(((f32[1,1024,512]{2,1,0:T(8,128)}), f32[4,1024,512]{2,1,0:T(8,128)}) %all-gather.8.cloned.1.call-update) | async-done | bytes 8388624 | tf_op jit(solution)/shard_map/all_gather | solution.py:15
  457.3 3.1 slice_bitcast_fusion
  460.5 22.8 %while.36 = (s32[]{:T(128)}, f32[1024,4]{0,1:T(4,128)S(1)}, f32[1024,4]{0,1:T(4,128)S(1)}, f32[1024,512]{1,0:T(8,128)}, f32[4,1024,4]{1,2,0:T(4,128)S(1)}, /*ind...) while((s32[]{:T(128)}, f32[1024,4]{0,1:T(4,128)S(1)}, ...), condition=%wide.region_5.6_spmd, body=%wide.region_4.5_spmd.sunk | while | flops 1597445 | bytes 14909591 | solution.py:21
  463.4 4.6 fusion.34
  471.0 4.6 fusion.34
  478.6 4.6 fusion.34
  (186 shorter events, 132.0 us)
Async XLA Ops:
  6.5 86.8 %all-gather.4.cloned.1.call-start = ((), (), s32[]{:S(2)}) async-start(), calls=%async_computation | async-start | bytes 4259840 | tf_op jit(solution)/shard_map/all_gather | solution.py:40
  7.3 165.1 %all-gather.6.cloned.1.call-start = ((), (), s32[]{:S(2)}) async-start(), calls=%async_computation.1 | async-start | bytes 4259840 | tf_op jit(solution)/shard_map/all_gather | solution.py:41
  8.0 449.3 %all-gather.8.cloned.1.call-start = ((), (), s32[]{:S(2)}) async-start(), calls=%async_computation.2 | async-start | bytes 10485760 | tf_op jit(solution)/shard_map/all_gather | solution.py:15
  185.4 3.2 copy-start
  210.6 3.2 copy-start
  235.8 3.2 copy-start
  261.1 3.2 copy-start
  286.3 3.2 copy-start
  311.5 3.2 copy-start
  336.7 3.2 copy-start
  361.9 3.2 copy-start
Sparse Core Ops, SparseCore 0:
  10.1 83.1 all-gather.3
  96.1 76.2 all-gather.5
  374.3 82.9 all-gather.7
where the time goes:
time: 494 us; the launch traced here: 492 us
  waiting for transfers between devices  229 us (46%)
  local copies, waits for them, and re-layouts  101 us (20%)
  other arithmetic  51.8 us (10%)
  matrix products  51.4 us (10%)
  loops' own time  26.3 us (5%)
  blocking collectives  19.5 us (4%)
  between operations  13.1 us (3%)
    all_gather x1, waiting for transfers between devices, shards(): lax.all_gather(key_cache, 'pb', axis=0, tiled=True)  85.3 us
    all_gather x1, waiting for transfers between devices, shards(): lax.all_gather(value_cache, 'pb', axis=0, tiled=True)  79.1 us
    all_gather x1, waiting for transfers between devices, merged(): everything = jax.tree.map(lambda part: lax.all_gather(part, axis), shard)  63.6 us
    dot_general x8, matrix products, one_block(): jnp.einsum('hqsk,skd->qhd', weights.astype(jnp.bfloat16), value_tiles, pr...  41.5 us
    another operation x1, loops' own time, shards(): lax.map(one_block, jnp.arange(local_blocks, dtype=jnp.int32))  26.2 us
    gather x8, local copies, waits for them, and re-layouts, one_block(): key_tiles = all_key_tiles[picked]  23.5 us
    gather x8, local copies, waits for them, and re-layouts, one_block(): value_tiles = all_value_tiles[picked]  23.5 us
    all_gather x2, blocking collectives, merged(): everything = jax.tree.map(lambda part: lax.all_gather(part, axis), shard)  19.5 us
  transfers between devices with their start and end apart: 3, of which 3 were waited for; matrix products, arithmetic and copies ran while one was open for 0% of the time, Pallas kernels for 0%

commit v1 on v0

--- a/solution.py
+++ b/solution.py
@@ -38,7 +38,9 @@
 def shards(queries, key_cache, value_cache, block_list, block_count):
     shard_keys, shard_values = (
         lax.all_gather(key_cache, "pb", axis=0, tiled=True),
-        lax.all_gather(value_cache, "pb", axis=0, tiled=True),
+        jnp.concatenate(
+            lax.all_to_all(jnp.stack([value_cache] * lax.axis_size("pb")), "pb", 0, 0), axis=0
+        ),
     )
     group_index = lax.axis_index("pb")
     shard_index = lax.axis_index("ka")

time: 494 us -> 449 us (0.909)
  waiting for transfers between devices: 229 us -> 173 us
  starting transfers between devices: 0.08 us -> 13.4 us
    all_gather x1 -> x0, waiting for transfers between devices: 79.1 us -> none  [shards(): lax.all_gather(value_cache, 'pb', axis=0, tiled=True)]
    all_to_all x0 -> x1, waiting for transfers between devices: none -> 16.6 us  [shards(): lax.all_to_all(jnp.stack([value_cache] * lax.axis_size('pb')), 'pb', 0, 0)]
    all_to_all x0 -> x1, starting transfers between devices: none -> 13.3 us  [shards(): lax.all_to_all(jnp.stack([value_cache] * lax.axis_size('pb')), 'pb', 0, 0)]
    dynamic_slice x8, local copies, waits for them, and re-layouts: 10.5 us -> 5.22 us  [one_block(): lax.dynamic_index_in_dim(block_count, block_pos, 0, keepdims=False)]
  transfers between devices with their start and end apart: 3 -> 3, of which waited for: 3 -> 3; matrix products, arithmetic and copies ran while one was open for 0% -> 1% of each run, Pallas kernels for 0% -> 0%
where the time goes in v1:
time: 449 us; the launch traced here: 447 us
  waiting for transfers between devices  173 us (39%)
  local copies, waits for them, and re-layouts  99.1 us (22%)
  other arithmetic  51.8 us (12%)
  matrix products  51.4 us (11%)
  loops' own time  26.3 us (6%)
  blocking collectives  19 us (4%)
  between operations  13.5 us (3%)
  starting transfers between devices  13.4 us (3%)
    all_gather x1, waiting for transfers between devices, shards(): lax.all_gather(key_cache, 'pb', axis=0, tiled=True)  90.1 us
    all_gather x1, waiting for transfers between devices, merged(): everything = jax.tree.map(lambda part: lax.all_gather(part, axis), shard)  65.2 us
    dot_general x8, matrix products, one_block(): jnp.einsum('hqsk,skd->qhd', weights.astype(jnp.bfloat16), value_tiles, pr...  41.5 us
    another operation x1, loops' own time, shards(): lax.map(one_block, jnp.arange(local_blocks, dtype=jnp.int32))  26.2 us
    gather x8, local copies, waits for them, and re-layouts, one_block(): key_tiles = all_key_tiles[picked]  23.5 us
    gather x8, local copies, waits for them, and re-layouts, one_block(): value_tiles = all_value_tiles[picked]  23.5 us
    all_gather x2, blocking collectives, merged(): everything = jax.tree.map(lambda part: lax.all_gather(part, axis), shard)  19 us
    all_to_all x1, waiting for transfers between devices, shards(): lax.all_to_all(jnp.stack([value_cache] * lax.axis_size('pb')), 'pb', 0, 0)  16.6 us
  transfers between devices with their start and end apart: 3, of which 3 were waited for; matrix products, arithmetic and copies ran while one was open for 1% of the time, Pallas kernels for 0%

profile of v1, /device:TPU:1, one launch (start us, length us, event | category | flops | bytes accessed | tf_op | source)
XLA Modules:
  0.0 446.9 jit_solution(2412707682118810137)
XLA Ops:
  7.3 3.8 stack.2
  11.1 13.3 %all-to-all-start = ((bf16[64,256,128]{2,1,0:T(8,128)(2,1)}), bf16[64,256,128]{2,1,0:T(8,128)(2,1)}, u32[]{:S(2)}, u32[]{:S(2)}) async-start(bf16[64,256,128]{2,1,0:T(8,128)(2,1)} %stack.2), calls=%async_computation | async-start | bytes 8388608 | tf_op jit(solution)/shard_map/all_to_all | solution.py:42
  24.5 90.1 %all-gather.3.cloned.1.call-done = bf16[16384,128]{1,0:T(8,128)(2,1)} async-done(((bf16[256,128]{1,0:T(8,128)(2,1)}), bf16[16384,128]{1,0:T(8,128)(2,1)}) %all-gather.3.cloned.1.call-update) | async-done | bytes 4194320 | tf_op jit(solution)/shard_map/all_gather | solution.py:40
  114.5 16.6 %all-to-all-done = bf16[64,256,128]{2,1,0:T(8,128)(2,1)} async-done(((bf16[64,256,128]{2,1,0:T(8,128)(2,1)}), bf16[64,256,128]{2,1,0:T(8,128)(2,1)}, u32[]{:S(2)}, u32[]{:S(2)}) %all-to-all-start) | async-done | bytes 4194336 | tf_op jit(solution)/shard_map/all_to_all | solution.py:42
  131.1 196.5 %while.37 = (s32[]{:T(128)}, f32[8,128,4]{1,2,0:T(4,128)S(1)}, f32[8,128,4]{1,2,0:T(4,128)S(1)}, f32[8,128,512]{2,1,0:T(8,128)}, s32[8]{0:T(128)S(1)}, /*index=5...) while((s32[]{:T(128)}, f32[8,128,4]{1,2,0:T(4,128)S(1)}, ...), condition=%wide.region_3.4_spmd.clone, body=%wide.region_0.3_spmd.clone.sunk | while | flops 1098400256 | bytes 69129872 | solution.py:89
  139.2 2.9 gather_fusion
  149.6 5.2 %fusion.41 = f32[128,4,128,1]{2,0,1,3:T(8,128)S(1)} fusion(f32[32,128,128,4]{2,1,3,0:T(8,128)} %copy-done, f32[4,128]{1,0:T(4,128)S(1)} %get-tuple-element.581, pred[128,32,128]{0,2,1:T(8,128)(4,1)S(1)} %or_and_fusion.2, bf16[32,128,128]{2,1,0:T(8,128)(2,1)S(1)} %gather_fusion.1), kind=kOutput, calls=%fused_computation.20.clone.1 | convolution fusion | flops 545259520 | bytes 10225664 | tf_op jit(solution)/shard_map/while/body/eval_jaxpr/hqsk,skd->qhd/dot_general | solution.py:81
  174.2 5.2 %fusion.41 = f32[128,4,128,1]{2,0,1,3:T(8,128)S(1)} fusion(f32[32,128,128,4]{2,1,3,0:T(8,128)} %copy-done, f32[4,128]{1,0:T(4,128)S(1)} %get-tuple-element.581, pred[128,32,128]{0,2,1:T(8,128)(4,1)S(1)} %or_and_fusion.2, bf16[32,128,128]{2,1,0:T(8,128)(2,1)S(1)} %gather_fusion.1), kind=kOutput, calls=%fused_computation.20.clone.1 | convolution fusion | flops 545259520 | bytes 10225664 | tf_op jit(solution)/shard_map/while/body/eval_jaxpr/hqsk,skd->qhd/dot_general | solution.py:81
  188.4 2.9 gather_fusion
  198.7 5.2 %fusion.41 = f32[128,4,128,1]{2,0,1,3:T(8,128)S(1)} fusion(f32[32,128,128,4]{2,1,3,0:T(8,128)} %copy-done, f32[4,128]{1,0:T(4,128)S(1)} %get-tuple-element.581, pred[128,32,128]{0,2,1:T(8,128)(4,1)S(1)} %or_and_fusion.2, bf16[32,128,128]{2,1,0:T(8,128)(2,1)S(1)} %gather_fusion.1), kind=kOutput, calls=%fused_computation.20.clone.1 | convolution fusion | flops 545259520 | bytes 10225664 | tf_op jit(solution)/shard_map/while/body/eval_jaxpr/hqsk,skd->qhd/dot_general | solution.py:81
  223.3 5.2 %fusion.41 = f32[128,4,128,1]{2,0,1,3:T(8,128)S(1)} fusion(f32[32,128,128,4]{2,1,3,0:T(8,128)} %copy-done, f32[4,128]{1,0:T(4,128)S(1)} %get-tuple-element.581, pred[128,32,128]{0,2,1:T(8,128)(4,1)S(1)} %or_and_fusion.2, bf16[32,128,128]{2,1,0:T(8,128)(2,1)S(1)} %gather_fusion.1), kind=kOutput, calls=%fused_computation.20.clone.1 | convolution fusion | flops 545259520 | bytes 10225664 | tf_op jit(solution)/shard_map/while/body/eval_jaxpr/hqsk,skd->qhd/dot_general | solution.py:81
  237.5 2.9 gather_fusion
  247.8 5.2 %fusion.41 = f32[128,4,128,1]{2,0,1,3:T(8,128)S(1)} fusion(f32[32,128,128,4]{2,1,3,0:T(8,128)} %copy-done, f32[4,128]{1,0:T(4,128)S(1)} %get-tuple-element.581, pred[128,32,128]{0,2,1:T(8,128)(4,1)S(1)} %or_and_fusion.2, bf16[32,128,128]{2,1,0:T(8,128)(2,1)S(1)} %gather_fusion.1), kind=kOutput, calls=%fused_computation.20.clone.1 | convolution fusion | flops 545259520 | bytes 10225664 | tf_op jit(solution)/shard_map/while/body/eval_jaxpr/hqsk,skd->qhd/dot_general | solution.py:81
  272.4 5.2 %fusion.41 = f32[128,4,128,1]{2,0,1,3:T(8,128)S(1)} fusion(f32[32,128,128,4]{2,1,3,0:T(8,128)} %copy-done, f32[4,128]{1,0:T(4,128)S(1)} %get-tuple-element.581, pred[128,32,128]{0,2,1:T(8,128)(4,1)S(1)} %or_and_fusion.2, bf16[32,128,128]{2,1,0:T(8,128)(2,1)S(1)} %gather_fusion.1), kind=kOutput, calls=%fused_computation.20.clone.1 | convolution fusion | flops 545259520 | bytes 10225664 | tf_op jit(solution)/shard_map/while/body/eval_jaxpr/hqsk,skd->qhd/dot_general | solution.py:81
  297.0 5.2 %fusion.41 = f32[128,4,128,1]{2,0,1,3:T(8,128)S(1)} fusion(f32[32,128,128,4]{2,1,3,0:T(8,128)} %copy-done, f32[4,128]{1,0:T(4,128)S(1)} %get-tuple-element.581, pred[128,32,128]{0,2,1:T(8,128)(4,1)S(1)} %or_and_fusion.2, bf16[32,128,128]{2,1,0:T(8,128)(2,1)S(1)} %gather_fusion.1), kind=kOutput, calls=%fused_computation.20.clone.1 | convolution fusion | flops 545259520 | bytes 10225664 | tf_op jit(solution)/shard_map/while/body/eval_jaxpr/hqsk,skd->qhd/dot_general | solution.py:81
  321.6 5.2 %fusion.41 = f32[128,4,128,1]{2,0,1,3:T(8,128)S(1)} fusion(f32[32,128,128,4]{2,1,3,0:T(8,128)} %copy-done, f32[4,128]{1,0:T(4,128)S(1)} %get-tuple-element.581, pred[128,32,128]{0,2,1:T(8,128)(4,1)S(1)} %or_and_fusion.2, bf16[32,128,128]{2,1,0:T(8,128)(2,1)S(1)} %gather_fusion.1), kind=kOutput, calls=%fused_computation.20.clone.1 | convolution fusion | flops 545259520 | bytes 10225664 | tf_op jit(solution)/shard_map/while/body/eval_jaxpr/hqsk,skd->qhd/dot_general | solution.py:81
  327.6 9.5 %all_gather.13 = f32[4,1024,4]{1,2,0:T(4,128)S(1)} all-gather(f32[1,1024,4]{1,2,0:T(4,128)S(1)} %bitcast.154), channel_id=1, replica_groups=mesh['pb'=64,'ka'=4] {'ka'}, dimensions={0}, use_global_device_ids=true | all-gather | bytes 81920 | tf_op jit(solution)/shard_map/all_gather | solution.py:15
  337.1 9.5 %all_gather.14 = f32[4,1024,4]{1,2,0:T(4,128)S(1)} all-gather(f32[1,1024,4]{1,2,0:T(4,128)S(1)} %bitcast.155), channel_id=1, replica_groups=mesh['pb'=64,'ka'=4] {'ka'}, dimensions={0}, use_global_device_ids=true | all-gather | bytes 81920 | tf_op jit(solution)/shard_map/all_gather | solution.py:15
  346.7 65.2 %all-gather.5.cloned.1.call-done = f32[4,1024,512]{2,1,0:T(8,128)} async-done(((f32[1,1024,512]{2,1,0:T(8,128)}), f32[4,1024,512]{2,1,0:T(8,128)}) %all-gather.5.cloned.1.call-update) | async-done | bytes 8388624 | tf_op jit(solution)/shard_map/all_gather | solution.py:15
  411.9 3.1 slice_bitcast_fusion
  415.0 22.8 %while.36 = (s32[]{:T(128)}, f32[1024,4]{0,1:T(4,128)S(1)}, f32[1024,4]{0,1:T(4,128)S(1)}, f32[1024,512]{1,0:T(8,128)}, f32[4,1024,4]{1,2,0:T(4,128)S(1)}, /*ind...) while((s32[]{:T(128)}, f32[1024,4]{0,1:T(4,128)S(1)}, ...), condition=%wide.region_5.6_spmd, body=%wide.region_4.5_spmd.sunk | while | flops 1597445 | bytes 14909591 | solution.py:21
  418.0 4.6 %fusion.34 = f32[1024,512]{1,0:T(8,128)} fusion(f32[128,8,4,128]{3,2,1,0:T(4,128)S(1)} %bitcast.147, f32[1024,512]{1,0:T(8,128)} %get-tuple-element.648, f32[128,8,4,128]{3,2,1,0:T(4,128)S(1)} %bitcast.148, f32[4,1024,512]{2,1,0:T(8,128)} %get-tuple-element.661, s32[]{:T(128)S(6)} %select_n.78), kind=kLoop, calls=%fused_computation.5.clone.1 | loop fusion | flops 1572864 | bytes 10485764 | tf_op jit(solution)/shard_map/while/body/eval_jaxpr/add | solution.py:32
  425.5 4.6 %fusion.34 = f32[1024,512]{1,0:T(8,128)} fusion(f32[128,8,4,128]{3,2,1,0:T(4,128)S(1)} %bitcast.147, f32[1024,512]{1,0:T(8,128)} %get-tuple-element.648, f32[128,8,4,128]{3,2,1,0:T(4,128)S(1)} %bitcast.148, f32[4,1024,512]{2,1,0:T(8,128)} %get-tuple-element.661, s32[]{:T(128)S(6)} %select_n.78), kind=kLoop, calls=%fused_computation.5.clone.1 | loop fusion | flops 1572864 | bytes 10485764 | tf_op jit(solution)/shard_map/while/body/eval_jaxpr/add | solution.py:32
  433.1 4.6 %fusion.34 = f32[1024,512]{1,0:T(8,128)} fusion(f32[128,8,4,128]{3,2,1,0:T(4,128)S(1)} %bitcast.147, f32[1024,512]{1,0:T(8,128)} %get-tuple-element.648, f32[128,8,4,128]{3,2,1,0:T(4,128)S(1)} %bitcast.148, f32[4,1024,512]{2,1,0:T(8,128)} %get-tuple-element.661, s32[]{:T(128)S(6)} %select_n.78), kind=kLoop, calls=%fused_computation.5.clone.1 | loop fusion | flops 1572864 | bytes 10485764 | tf_op jit(solution)/shard_map/while/body/eval_jaxpr/add | solution.py:32
  (188 shorter events, 132.0 us)
Async XLA Ops:
  6.5 108.0 %all-gather.3.cloned.1.call-start = ((), (), s32[]{:S(2)}) async-start(), calls=%async_computation.1 | async-start | bytes 4259840 | tf_op jit(solution)/shard_map/all_gather | solution.py:40
  11.1 120.0 %copy-start.1 = (s32[8]{0:T(128)S(1)}, s32[8]{0:T(128)}, u32[]{:S(2)}) copy-start(s32[8]{0:T(128)} %param.13) | copy-start | bytes 100
  11.1 120.0 %all-to-all-start = ((bf16[64,256,128]{2,1,0:T(8,128)(2,1)}), bf16[64,256,128]{2,1,0:T(8,128)(2,1)}, u32[]{:S(2)}, u32[]{:S(2)}) async-start(bf16[64,256,128]{2,1,0:T(8,128)(2,1)} %stack.2), calls=%async_computation | async-start | bytes 8388608 | tf_op jit(solution)/shard_map/all_to_all | solution.py:42
  24.4 387.5 %all-gather.5.cloned.1.call-start = ((), (), s32[]{:S(2)}) async-start(), calls=%async_computation.2 | async-start | bytes 10485760 | tf_op jit(solution)/shard_map/all_gather | solution.py:15
  143.4 3.2 copy-start
  168.0 3.2 copy-start
  192.6 3.2 copy-start
  217.1 3.2 copy-start
  241.7 3.2 copy-start
  266.2 3.2 copy-start
  290.8 3.2 copy-start
  315.4 3.2 copy-start
Sparse Core Ops, SparseCore 0:
  10.1 104.3 all-gather.2
  327.8 84.0 all-gather.4
